TPU v7x, 768 devices: a whole 4x8x12 slice. The times are simulated.
768 devices in a mesh: gx: 96 (over x, y, z_hi), gy: 8 (over z_lo, core).
Axes of the slice: x: 4, y: 8, z: 12 (z_hi: 3, z_lo: 4; z = z_hi * 4 + z_lo), core: 2. Of those that a mesh axis runs over, the one named last changes fastest.
Arguments:
- state: float32 [54, 768, 8192], P(None, 'gx', 'gy'), may hold values from 0.05 to 3, as said below
- diffusivity: float32 [54], replicated, may hold values from 0.02 to 0.1
- log_prefactor: float32 [325], replicated, may hold values from -1 to 1
- activation: float32 [325], replicated, may hold values from 0.5 to 4
- heat: float32 [325], replicated, may hold values from 0.005 to 0.05
- reactants: float32 [650, 53], replicated, may hold values from 0 to 1, as said below
- products: float32 [53, 325], replicated, may hold values from 0 to 2, as said below
- substeps: int32 [768, 64], P('gx', 'gy'), may hold values from 1 to 4
- flame: int32 [768, 64], P('gx', 'gy'), may hold values from 0 to 1, as said below
Outputs:
- next_state: float32 [54, 768, 8192], P(None, 'gx', 'gy')
Inputs may be any that keep to these rules, and one draw needn't show every extreme that they name: `state`: component 0 is the temperature, from 1 to 3; the other components are concentrations from 0.05 to 2. `reactants`: each row is one-hot: it names one species. `products`: column r is the sum of two one-hot columns, the two products of reaction r. `flame`: within the 8 x (8) entries that one device holds, at most 8 are 1. In every draw there is one index along the first mesh axis where every device holds exactly 8; elsewhere a device holds 8 with probability 1/4 and otherwise 0 to 2.
All inputs are finite; a program needn't handle non-finite values.
Results may differ from a plain program's by a relative error of at most 0.0001.
Values sent between devices are 32-bit elements; how exact they have to be, the bound alone decides.
A program may use at most 128 MiB of HBM per device.

v0:
```python
import jax
import jax.numpy as jnp
from jax import lax
from jax.sharding import PartitionSpec as P

NZ = 32
BLOCK = 128


near_weight = 4.0 / 3.0
far_weight = 1.0 / 12.0
centre_weight = 7.5
slot_group = 4


def extended(block, sides, width):
    for axis, dim in sides:
        count = lax.axis_size(axis)
        forward = [(i, i + 1) for i in range(count - 1)]
        forward.append((count - 1, 0))
        backward = [(target, source) for source, target in forward]
        low = lax.ppermute(
            lax.slice_in_dim(block, block.shape[dim] - width, None, axis=dim), axis, forward
        )
        high = lax.ppermute(lax.slice_in_dim(block, 0, width, axis=dim), axis, backward)
        block = jnp.concatenate([low, block, high], axis=dim)
    return block


def along_z(field, offset, zposition):
    if offset > 0:
        return jnp.where(
            zposition < NZ - offset, jnp.roll(field, -offset, -1), jnp.roll(field, NZ - offset, -1)
        )
    reach = -offset
    return jnp.where(
        zposition >= reach, jnp.roll(field, reach, -1), jnp.roll(field, reach - NZ, -1)
    )


def react_step(thermal, amounts, step_size, log_prefactor, activation, heat, reactants, products):
    exact_result = lax.Precision.HIGHEST
    nreact = log_prefactor.shape[0]
    speeds = jnp.exp(log_prefactor[:, None] - activation[:, None] / thermal[..., None, :])
    picked = jnp.einsum("qs,...sn->...qn", reactants, amounts, precision=exact_result)
    first_side = picked[..., :nreact, :]
    second_side = picked[..., nreact:, :]
    progress = speeds * first_side * second_side
    produced = jnp.einsum("sr,...rn->...sn", products, progress, precision=exact_result)
    partner = jnp.concatenate([speeds * second_side, speeds * first_side], axis=-2)
    consumed = jnp.einsum("qs,...qn->...sn", reactants, partner, precision=exact_result)
    widened = step_size[..., None, :]
    new_amounts = (amounts + widened * produced) / (1.0 + widened * consumed)
    new_thermal = thermal + step_size * jnp.einsum(
        "r,...rn->...n", heat, progress, precision=exact_result
    )
    return (new_thermal, new_amounts)


def react_slots(reaction_slots, slot_counts, log_prefactor, activation, heat, reactants, products):
    ranking = jnp.argsort(-slot_counts, stable=True)
    ranked = reaction_slots[ranking]
    ranked_counts = slot_counts[ranking]
    pieces = []
    for start_at in range(0, reaction_slots.shape[0], slot_group):
        cluster = ranked[start_at : start_at + slot_group]
        cluster_counts = ranked_counts[start_at : start_at + slot_group]
        step_size = (1.0 / jnp.maximum(cluster_counts, 1).astype(jnp.float32))[:, None]

        def advance(substep, carry, cluster_counts=cluster_counts, step_size=step_size):
            thermal, amounts = carry
            new_thermal, new_amounts = react_step(
                thermal, amounts, step_size, log_prefactor, activation, heat, reactants, products
            )
            active = substep < cluster_counts
            return (
                jnp.where(active[:, None], new_thermal, thermal),
                jnp.where(active[:, None, None], new_amounts, amounts),
            )

        thermal, amounts = lax.fori_loop(
            0, cluster_counts[0], advance, (cluster[:, 0], cluster[:, 1:])
        )
        pieces.append(jnp.concatenate([thermal[:, None], amounts], 1))
    merged = jnp.concatenate(pieces, 0)
    return merged[jnp.argsort(ranking)]


def per_device(
    state, diffusivity, log_prefactor, activation, heat, reactants, products, substeps, flame
):
    exact_result = lax.Precision.HIGHEST
    components, planes, row_cells = state.shape
    zposition = jnp.arange(row_cells) % NZ
    wide_x = extended(state, (("gx", 1),), 2)
    wide_y = extended(state, (("gy", 2),), 2 * NZ)
    nearest = wide_x[:, 1 : planes + 1] + wide_x[:, 3 : planes + 3]
    nearest = (
        nearest + wide_y[:, :, NZ : NZ + row_cells] + wide_y[:, :, 3 * NZ : 3 * NZ + row_cells]
    )
    nearest = nearest + along_z(state, 1, zposition) + along_z(state, -1, zposition)
    farther = wide_x[:, 0:planes] + wide_x[:, 4 : planes + 4]
    farther = farther + wide_y[:, :, 0:row_cells] + wide_y[:, :, 4 * NZ : 4 * NZ + row_cells]
    farther = farther + along_z(state, 2, zposition) + along_z(state, -2, zposition)
    transport = diffusivity[:, None, None] * (
        near_weight * nearest - far_weight * farther - centre_weight * state
    )
    block_list = state.reshape(components, -1, BLOCK)
    burning = flame.reshape(-1)
    work_counts = (flame * substeps).reshape(-1)
    burn_rank = jnp.cumsum(burning) - burning
    adjacent_cells = lax.axis_size("gy")
    slot_ids = jnp.arange(adjacent_cells, dtype=jnp.int32)
    picker = (burn_rank[None, :] == slot_ids[:, None]) & (burning[None, :] == 1)
    select_float_value = picker.astype(jnp.float32)
    reaction_slots = jnp.einsum(
        "vi,gik->vgk", select_float_value, block_list, precision=exact_result
    )
    slot_counts = jnp.sum(jnp.where(picker, work_counts[None, :], 0), axis=1)
    completed_blocks = react_slots(
        reaction_slots, slot_counts, log_prefactor, activation, heat, reactants, products
    )
    spread_amount = jnp.einsum(
        "uw,uxy->xwy", select_float_value, completed_blocks, precision=exact_result
    )
    reacted = jnp.where(burning[None, :, None] == 1, spread_amount, block_list).reshape(state.shape)
    return reacted + transport


def solution(mesh):
    in_specs = (P(None, "gx", "gy"), P(), P(), P(), P(), P(), P(), P("gx", "gy"), P("gx", "gy"))
    out_specs = P(None, "gx", "gy")
    return jax.shard_map(
        per_device, mesh=mesh, in_specs=in_specs, out_specs=out_specs, check_vma=False
    )
```

profile of v0, /device:TPU:67, one launch (start us, length us, event | category | flops | bytes accessed | tf_op | source)
XLA Modules:
  0.0 107.4 jit_solution(606885056521756115)
XLA Ops:
  0.0 2.6 %fusion.87 = (f32[54,2,1024]{2,1,0:T(2,128)S(1)}, f32[54,2,1024]{2,1,0:T(2,128)S(1)}) fusion(f32[54,8,1024]{2,1,0:T(8,128)} %param.13), kind=kLoop, calls=%fused_computation.121 | loop fusion | bytes 1769472 | tf_op jit(solution)/shard_map/slice | solution.py:25
  3.6 16.2 %collective-permute-start.1 = (f32[54,2,1024]{2,0,1:T(8,128)}, f32[54,2,1024]{2,0,1:T(8,128)}, u32[]{:S(2)}, u32[]{:S(2)}) collective-permute-start(f32[54,2,1024]{2,0,1:T(8,128)} %copy.27), channel_id=1, source_target_pairs={{8,0},{16,8},{24,16},{32,24},{40,32},{48,40},{56,48},{64,56},{72,6... | collective-permute-start | bytes 1327112 | tf_op jit(solution)/shard_map/ppermute | solution.py:25
  20.6 2.9 %collective-permute-start.3 = (f32[54,8,64]{2,1,0:T(8,128)}, f32[54,8,64]{2,1,0:T(8,128)}, u32[]{:S(2)}, u32[]{:S(2)}) collective-permute-start(f32[54,8,64]{2,1,0:T(8,128)} %get-tuple-element.237), channel_id=1, source_target_pairs={{1,0},{2,1},{3,2},{4,3},{5,4},{6,5},{7,6},{0,7},{9,8},{10,9},{11,1... | collective-permute-start | bytes 331784 | tf_op jit(solution)/shard_map/ppermute | solution.py:25
  24.4 1.9 %collective-permute-start = (f32[54,2,1024]{2,0,1:T(8,128)}, f32[54,2,1024]{2,0,1:T(8,128)}, u32[]{:S(2)}, u32[]{:S(2)}) collective-permute-start(f32[54,2,1024]{2,0,1:T(8,128)} %copy.26), channel_id=1, source_target_pairs={{0,8},{8,16},{16,24},{24,32},{32,40},{40,48},{48,56},{56,64},{64,7... | collective-permute-start | bytes 1327112 | tf_op jit(solution)/shard_map/ppermute | solution.py:22
  26.3 3.0 %collective-permute-start.2 = (f32[54,8,64]{2,1,0:T(8,128)}, f32[54,8,64]{2,1,0:T(8,128)}, u32[]{:S(2)}, u32[]{:S(2)}) collective-permute-start(f32[54,8,64]{2,1,0:T(8,128)} %get-tuple-element.238), channel_id=1, source_target_pairs={{0,1},{1,2},{2,3},{3,4},{4,5},{5,6},{6,7},{7,0},{8,9},{9,10},{10,1... | collective-permute-start | bytes 331784 | tf_op jit(solution)/shard_map/ppermute | solution.py:22
  33.4 1.5 %reshape.77 = f32[54,64,128]{2,1,0:T(8,128)} reshape(f32[54,8,1024]{2,1,0:T(8,128)S(1)} %copy-done) | data formatting | bytes 3538944 | tf_op jit(solution)/shard_map/reshape | solution.py:108
  34.9 2.2 %fusion.73 = f32[8,54,128]{2,0,1:T(8,128)S(1)} fusion(f32[54,64,128]{2,1,0:T(8,128)} %reshape.77, s32[64]{0:T(128)S(1)} %sub.29, pred[64]{0:T(512)(128)(4,1)S(1)} %broadcast_compare_fusion.2), kind=kOutput, calls=%fused_computation.103 | convolution fusion | flops 42468352 | bytes 1990976 | tf_op jit(solution)/shard_map/vi,gik->vgk/dot_general | solution.py:116
  37.7 2.6 %fusion.79 = (f32[54,8,994]{2,1,0:T(8,128)}, f32[54,8,994]{2,1,0:T(8,128)}) fusion(f32[54,8,1024]{2,1,0:T(8,128)S(1)} %copy-done), kind=kLoop, calls=%fused_computation.113 | loop fusion | bytes 6870528 | tf_op jit(solution)/shard_map/jit(_roll_static)/slice | solution.py:37
  40.3 2.6 %fusion.82 = (f32[54,8,1022]{2,1,0:T(8,128)}, f32[54,8,1022]{2,1,0:T(8,128)}) fusion(f32[54,8,1024]{2,1,0:T(8,128)S(1)} %copy-done), kind=kLoop, calls=%fused_computation.116 | loop fusion | bytes 7064064 | tf_op jit(solution)/shard_map/jit(_roll_static)/slice | solution.py:37
  42.8 2.5 %fusion.83 = (f32[54,8,993]{2,1,0:T(8,128)}, f32[54,8,993]{2,1,0:T(8,128)}) fusion(f32[54,8,1024]{2,1,0:T(8,128)S(1)} %copy-done), kind=kLoop, calls=%fused_computation.117 | loop fusion | bytes 6863616 | tf_op jit(solution)/shard_map/jit(_roll_static)/slice | solution.py:37
  45.3 2.5 %fusion.86 = (f32[54,8,1023]{2,1,0:T(8,128)}, f32[54,8,1023]{2,1,0:T(8,128)}) fusion(f32[54,8,1024]{2,1,0:T(8,128)S(1)} %copy-done), kind=kLoop, calls=%fused_computation.120 | loop fusion | bytes 7070976 | tf_op jit(solution)/shard_map/jit(_roll_static)/slice | solution.py:37
  51.1 19.3 %while.26 = (s32[]{:T(128)}, f32[4,128]{1,0:T(4,128)S(1)}, f32[4,53,128]{2,1,0:T(8,128)S(1)}, s32[]{:T(128)}, s32[4]{0:T(128)S(1)}, /*index=5*/f32[4,1]{0,1:T(1,...) while((s32[]{:T(128)}, f32[4,128]{1,0:T(4,128)S(1)}, ...), condition=%wide.wide.region_4.5_spmd, body=%wide.wide.region_3.4_spmd.sunk | while | flops 532644352 | bytes 8943993 | solution.py:81
  51.8 1.3 %convolution_bitcast_fusion.6 = f32[4,650,128]{2,1,0:T(8,128)S(1)} fusion(f32[4,53,128]{2,1,0:T(8,128)S(1)} %get-tuple-element.583, f32[650,53]{0,1:T(8,128)S(1)} %get-tuple-element.603), kind=kOutput, calls=%fused_computation.3.clone.clone.1 | convolution fusion | flops 211660800 | bytes 1577544 | tf_op jit(solution)/shard_map/while/body/qs,...sn->...qn/dot_general | solution.py:45
  56.4 1.3 %convolution_bitcast_fusion.6 = f32[4,650,128]{2,1,0:T(8,128)S(1)} fusion(f32[4,53,128]{2,1,0:T(8,128)S(1)} %get-tuple-element.583, f32[650,53]{0,1:T(8,128)S(1)} %get-tuple-element.603), kind=kOutput, calls=%fused_computation.3.clone.clone.1 | convolution fusion | flops 211660800 | bytes 1577544 | tf_op jit(solution)/shard_map/while/body/qs,...sn->...qn/dot_general | solution.py:45
  61.1 1.3 %convolution_bitcast_fusion.6 = f32[4,650,128]{2,1,0:T(8,128)S(1)} fusion(f32[4,53,128]{2,1,0:T(8,128)S(1)} %get-tuple-element.583, f32[650,53]{0,1:T(8,128)S(1)} %get-tuple-element.603), kind=kOutput, calls=%fused_computation.3.clone.clone.1 | convolution fusion | flops 211660800 | bytes 1577544 | tf_op jit(solution)/shard_map/while/body/qs,...sn->...qn/dot_general | solution.py:45
  70.4 15.0 %while.27 = (s32[]{:T(128)}, f32[4,128]{1,0:T(4,128)S(1)}, f32[4,53,128]{2,1,0:T(8,128)S(1)}, s32[]{:T(128)}, s32[4]{0:T(128)S(1)}, /*index=5*/f32[4,1]{0,1:T(1,...) while((s32[]{:T(128)}, f32[4,128]{1,0:T(4,128)S(1)}, ...), condition=%wide.wide.region_6.7_spmd, body=%wide.wide.region_5.6_spmd.sunk | while | flops 532644352 | bytes 8943993 | solution.py:81
  71.3 1.3 %convolution_bitcast_fusion.7 = f32[4,650,128]{2,1,0:T(8,128)S(1)} fusion(f32[4,53,128]{2,1,0:T(8,128)S(1)} %get-tuple-element.541, f32[650,53]{0,1:T(8,128)S(1)} %get-tuple-element.561), kind=kOutput, calls=%fused_computation.28.clone.clone.1 | convolution fusion | flops 211660800 | bytes 1577544 | tf_op jit(solution)/shard_map/while/body/qs,...sn->...qn/dot_general | solution.py:45
  76.0 1.3 %convolution_bitcast_fusion.7 = f32[4,650,128]{2,1,0:T(8,128)S(1)} fusion(f32[4,53,128]{2,1,0:T(8,128)S(1)} %get-tuple-element.541, f32[650,53]{0,1:T(8,128)S(1)} %get-tuple-element.561), kind=kOutput, calls=%fused_computation.28.clone.clone.1 | convolution fusion | flops 211660800 | bytes 1577544 | tf_op jit(solution)/shard_map/while/body/qs,...sn->...qn/dot_general | solution.py:45
  80.7 1.3 %convolution_bitcast_fusion.7 = f32[4,650,128]{2,1,0:T(8,128)S(1)} fusion(f32[4,53,128]{2,1,0:T(8,128)S(1)} %get-tuple-element.541, f32[650,53]{0,1:T(8,128)S(1)} %get-tuple-element.561), kind=kOutput, calls=%fused_computation.28.clone.clone.1 | convolution fusion | flops 211660800 | bytes 1577544 | tf_op jit(solution)/shard_map/while/body/qs,...sn->...qn/dot_general | solution.py:45
  86.0 3.6 %bitcast_select_fusion = f32[54,64,128]{2,1,0:T(8,128)} fusion(f32[54,64,128]{2,1,0:T(8,128)} %reshape.77, pred[64]{0:T(512)(128)(4,1)S(1)} %broadcast_compare_fusion.2, f32[8,54,128]{2,1,0:T(8,128)S(1)} %gather_fusion.2, s32[64]{0:T(128)S(1)} %sub.29), kind=kOutput, calls=%fused_computation.81 | convolution fusion | flops 42910720 | bytes 3760448 | tf_op jit(solution)/shard_map/uw,uxy->xwy/dot_general | solution.py:123
  89.6 2.6 %reshape.78 = f32[54,8,1024]{2,1,0:T(8,128)} reshape(f32[54,64,128]{2,1,0:T(8,128)} %bitcast_select_fusion) | data formatting | bytes 3538944 | tf_op jit(solution)/shard_map/reshape | solution.py:126
  93.8 2.3 %copy_dynamic-update-slice_fusion = f32[54,10,1024]{2,1,0:T(8,128)S(1)} fusion(f32[54,10,1024]{2,1,0:T(8,128)S(1)} %get-tuple-element.235, f32[54,2,1024]{2,0,1:T(8,128)} %collective-permute-done.1), kind=kLoop, calls=%fused_computation.82 | loop fusion | bytes 884736 | tf_op jit(solution)/shard_map/concatenate | solution.py:26
  96.0 2.1 %copy.21 = f32[54,2,1024]{2,1,0:T(2,128)} copy(f32[54,2,1024]{2,0,1:T(8,128)} %collective-permute-done) | data formatting | bytes 884736 | tf_op jit(solution)/shard_map/ppermute | solution.py:22
  98.2 9.0 %fusion.55 = f32[54,8,1024]{2,1,0:T(8,128)} fusion(f32[54,8,1024]{2,1,0:T(8,128)} %reshape.78, f32[54,8,64]{2,1,0:T(8,128)} %collective-permute-done.2, f32[54,8,1024]{2,1,0:T(8,128)S(1)} %copy-done, f32[54,2,1024]{2,1,0:T(2,128)} %copy.21, f32[54,8,1088]{2,1,0:T(8,128)S(1)} %constant_dynamic-update-slice_fusion.1, ...), kind=kLoop, calls=%fused_computation.66 | loop fusion | flops 14598144 | bytes 27099352 | tf_op jit(solution)/shard_map/add | solution.py:127
  (115 shorter events, 33.0 us)
Async XLA Ops:
  0.0 19.8 %copy-start = (f32[54,8,1024]{2,1,0:T(8,128)S(1)}, f32[54,8,1024]{2,1,0:T(8,128)}, u32[]{:S(2)}) copy-start(f32[54,8,1024]{2,1,0:T(8,128)} %param.13) | copy-start | bytes 5308420
  2.6 26.7 %copy-start.10 = (s32[8,8]{1,0:T(8,128)S(1)}, s32[8,8]{1,0:T(8,128)}, u32[]{:S(2)}) copy-start(s32[8,8]{1,0:T(8,128)} %param.21) | copy-start | bytes 772
  2.6 27.1 %copy-start.12 = (s32[8,8]{1,0:T(8,128)S(1)}, s32[8,8]{1,0:T(8,128)}, u32[]{:S(2)}) copy-start(s32[8,8]{1,0:T(8,128)} %param.20) | copy-start | bytes 772
  3.6 90.2 %collective-permute-start.1 = (f32[54,2,1024]{2,0,1:T(8,128)}, f32[54,2,1024]{2,0,1:T(8,128)}, u32[]{:S(2)}, u32[]{:S(2)}) collective-permute-start(f32[54,2,1024]{2,0,1:T(8,128)} %copy.27), channel_id=1, source_target_pairs={{8,0},{16,8},{24,16},{32,24},{40,32},{48,40},{56,48},{64,56},{72,6... | collective-permute-start | bytes 1327112 | tf_op jit(solution)/shard_map/ppermute | solution.py:25
  20.6 72.0 %collective-permute-start.3 = (f32[54,8,64]{2,1,0:T(8,128)}, f32[54,8,64]{2,1,0:T(8,128)}, u32[]{:S(2)}, u32[]{:S(2)}) collective-permute-start(f32[54,8,64]{2,1,0:T(8,128)} %get-tuple-element.237), channel_id=1, source_target_pairs={{1,0},{2,1},{3,2},{4,3},{5,4},{6,5},{7,6},{0,7},{9,8},{10,9},{11,1... | collective-permute-start | bytes 331784 | tf_op jit(solution)/shard_map/ppermute | solution.py:25
  24.4 71.6 %collective-permute-start = (f32[54,2,1024]{2,0,1:T(8,128)}, f32[54,2,1024]{2,0,1:T(8,128)}, u32[]{:S(2)}, u32[]{:S(2)}) collective-permute-start(f32[54,2,1024]{2,0,1:T(8,128)} %copy.26), channel_id=1, source_target_pairs={{0,8},{8,16},{16,24},{24,32},{32,40},{40,48},{48,56},{56,64},{64,7... | collective-permute-start | bytes 1327112 | tf_op jit(solution)/shard_map/ppermute | solution.py:22
  26.3 71.9 %collective-permute-start.2 = (f32[54,8,64]{2,1,0:T(8,128)}, f32[54,8,64]{2,1,0:T(8,128)}, u32[]{:S(2)}, u32[]{:S(2)}) collective-permute-start(f32[54,8,64]{2,1,0:T(8,128)} %get-tuple-element.238), channel_id=1, source_target_pairs={{0,1},{1,2},{2,3},{3,4},{4,5},{5,6},{6,7},{7,0},{8,9},{9,10},{10,1... | collective-permute-start | bytes 331784 | tf_op jit(solution)/shard_map/ppermute | solution.py:22
  34.9 2.8 %copy-start.11 = (f32[325]{0:T(512)S(1)}, f32[325]{0:T(512)}, u32[]{:S(2)}) copy-start(f32[325]{0:T(512)} %param.17) | copy-start | bytes 3904
  47.8 3.3 %copy-start.1 = (f32[650,53]{0,1:T(8,128)S(1)}, f32[650,53]{0,1:T(8,128)}, u32[]{:S(2)}) copy-start(f32[650,53]{0,1:T(8,128)} %param.18) | copy-start | bytes 413404
  47.8 3.3 %copy-start.2 = (f32[53,325]{1,0:T(8,128)S(1)}, f32[53,325]{1,0:T(8,128)}, u32[]{:S(2)}) copy-start(f32[53,325]{1,0:T(8,128)} %param.19) | copy-start | bytes 206704
  47.8 3.3 %copy-start.8 = (f32[325]{0:T(512)S(1)}, f32[325]{0:T(512)}, u32[]{:S(2)}) copy-start(f32[325]{0:T(512)} %param.15) | copy-start | bytes 3904
  47.8 3.3 %copy-start.9 = (f32[325]{0:T(512)S(1)}, f32[325]{0:T(512)}, u32[]{:S(2)}) copy-start(f32[325]{0:T(512)} %param.16) | copy-start | bytes 3904
  92.2 5.9 %copy-start.4 = (f32[54,8,994]{2,1,0:T(8,128)S(1)}, f32[54,8,994]{2,1,0:T(8,128)}, u32[]{:S(2)}) copy-start(f32[54,8,994]{2,1,0:T(8,128)} %get-tuple-element.218) | copy-start | bytes 5152900
  92.3 5.9 %copy-start.5 = (f32[54,8,1022]{2,1,0:T(8,128)S(1)}, f32[54,8,1022]{2,1,0:T(8,128)}, u32[]{:S(2)}) copy-start(f32[54,8,1022]{2,1,0:T(8,128)} %get-tuple-element.223) | copy-start | bytes 5298052
  92.3 5.9 %copy-start.6 = (f32[54,8,1022]{2,1,0:T(8,128)S(1)}, f32[54,8,1022]{2,1,0:T(8,128)}, u32[]{:S(2)}) copy-start(f32[54,8,1022]{2,1,0:T(8,128)} %get-tuple-element.224) | copy-start | bytes 5298052
  92.6 5.6 %copy-start.3 = (f32[54,8,994]{2,1,0:T(8,128)S(1)}, f32[54,8,994]{2,1,0:T(8,128)}, u32[]{:S(2)}) copy-start(f32[54,8,994]{2,1,0:T(8,128)} %get-tuple-element.217) | copy-start | bytes 5152900
  92.6 5.6 %copy-start.7 = (f32[54,8,30]{2,1,0:T(8,128)S(1)}, f32[54,8,30]{2,1,0:T(8,128)}, u32[]{:S(2)}) copy-start(f32[54,8,30]{2,1,0:T(8,128)} %get-tuple-element.219) | copy-start | bytes 155524
  92.6 5.6 %copy-start.13 = (f32[54]{0:T(128)S(1)}, f32[54]{0:T(128)}, u32[]{:S(2)}) copy-start(f32[54]{0:T(128)} %param.14) | copy-start | bytes 652
where the time goes:
time: 108 us; the launch traced here: 107 us
  local copies, waits for them, and re-layouts  31.4 us (29%)
  matrix products  31.2 us (29%)
  starting transfers between devices  24 us (22%)
  other arithmetic  13.7 us (13%)
  loops' own time  6.51 us (6%)
    ppermute x2, starting transfers between devices, extended(): lax.ppermute(lax.slice_in_dim(block, 0, width, axis=dim), axis, backward)  19.1 us
    add x1, other arithmetic, per_device(): return reacted + transport  8.99 us
    dot_general x7, matrix products, react_step(): jnp.einsum('qs,...sn->...qn', reactants, amounts, precision=exact_result)  8.78 us
    dot_general x7, matrix products, react_step(): jnp.einsum('qs,...qn->...sn', reactants, partner, precision=exact_result)  7.69 us
    slice x4, local copies, waits for them, and re-layouts, along_z(): jnp.roll(field, reach - NZ, -1)  6.69 us
    slice x4, local copies, waits for them, and re-layouts, along_z(): jnp.roll(field, reach, -1)  6.68 us
    another operation x2, loops' own time, react_slots(): lax.fori_loop(0, cluster_counts[0], advance, (cluster[:, 0], cluster[:, 1...  6.51 us
    dot_general x7, matrix products, react_step(): jnp.einsum('sr,...rn->...sn', products, progress, precision=exact_result)  5 us
  transfers between devices with their start and end apart: 4, of which 0 were waited for; matrix products, arithmetic and copies ran while one was open for 59% of the time, Pallas kernels for 0%

commit v1 on v0

v1 whole, which is shorter than its diff:
```python
import functools

import jax
import jax.numpy as jnp
from jax import lax
from jax.experimental import pallas as pl
from jax.experimental.pallas import tpu as pltpu
from jax.sharding import PartitionSpec as P

NZ = 32
BLOCK = 128
MAXSUB = 4
SLOTS = 8
SP = 53
COMP = 54
RX = 325
CROWS = 64
RROWS = 336
RPAD = 384
WIDE = 256
HALF = COMP // 2
CHUNKS = ((0, 9), (9, 9), (18, 9), (27, 9), (36, 9), (45, 9))

near_weight = 4.0 / 3.0
far_weight = 1.0 / 12.0
centre_weight = 7.5

MESH = pl.DeviceIdType.MESH
F32 = jnp.float32
BF16 = jnp.bfloat16


def split2(x):
    high = x.astype(BF16)
    return high, (x - high.astype(F32)).astype(BF16)


def split3(x):
    high = x.astype(BF16)
    rest = x - high.astype(F32)
    middle = rest.astype(BF16)
    return high, middle, (rest - middle.astype(F32)).astype(BF16)


def kernel(
    n, m,
    state, diffusivity, log_prefactor, activation, heat, reactants_t, products, substeps, flame,
    out,
    S, H, YS, YR, DF, LP, AC, HT, RT, PT, SB, FL,
    LB, AB, RA, RB, C, PP, A, Q, CN, ST, Z, LV, RK,
    x_send, x_recv, y_send, y_recv, local,
):
    gx, gy = lax.axis_index("gx"), lax.axis_index("gy")
    right, left = lax.rem(gx + 1, n), lax.rem(gx + n - 1, n)
    up, down = lax.rem(gy + 1, m), lax.rem(gy + m - 1, m)

    barrier = pltpu.get_barrier_semaphore()
    for device in ((right, gy), (left, gy), (gx, up), (gx, down)):
        pl.semaphore_signal(barrier, inc=1, device_id=device, device_id_type=MESH)

    loads = [
        pltpu.make_async_copy(state, S, local.at[0]),
        pltpu.make_async_copy(diffusivity, DF, local.at[1]),
        pltpu.make_async_copy(log_prefactor, LP, local.at[2]),
        pltpu.make_async_copy(activation, AC, local.at[3]),
        pltpu.make_async_copy(heat, HT, local.at[4]),
        pltpu.make_async_copy(reactants_t, RT, local.at[5]),
        pltpu.make_async_copy(products, PT, local.at[6]),
        pltpu.make_async_copy(substeps, SB, local.at[7]),
        pltpu.make_async_copy(flame, FL, local.at[8]),
    ]
    for load in loads:
        load.start()

    pl.semaphore_wait(barrier, 4)
    x_copies = []
    for k, (c0, cn) in enumerate(CHUNKS):
        pair = (
            pltpu.make_async_remote_copy(
                state.at[c0 : c0 + cn, 6:8, :], H.at[c0 : c0 + cn, 6:8, :],
                x_send.at[0, k], x_recv.at[0, k], device_id=(right, gy), device_id_type=MESH,
            ),
            pltpu.make_async_remote_copy(
                state.at[c0 : c0 + cn, 0:2, :], H.at[c0 : c0 + cn, 0:2, :],
                x_send.at[1, k], x_recv.at[1, k], device_id=(left, gy), device_id_type=MESH,
            ),
        )
        for copy in pair:
            copy.start()
        x_copies.append(pair)
    loads[0].wait()
    lane = lax.broadcasted_iota(jnp.int32, (8, BLOCK), 1)
    sub = lax.broadcasted_iota(jnp.int32, (8, BLOCK), 0)

    def pack(c, _):
        YS[0, c] = jnp.where(
            lane < 64,
            pltpu.roll(S[c, :, 896:1024], 64, 1),
            S[c + HALF, :, 896:1024],
        )
        YS[1, c] = jnp.where(
            lane < 64,
            S[c, :, 0:128],
            pltpu.roll(S[c + HALF, :, 0:128], 64, 1),
        )
        return 0

    lax.fori_loop(0, HALF, pack, 0)

    y_copies = [
        pltpu.make_async_remote_copy(
            YS.at[0], YR.at[0], y_send.at[0], y_recv.at[0], device_id=(gx, up), device_id_type=MESH
        ),
        pltpu.make_async_remote_copy(
            YS.at[1], YR.at[1], y_send.at[1], y_recv.at[1], device_id=(gx, down), device_id_type=MESH
        ),
    ]
    for copy in y_copies:
        copy.start()

    for load in loads[1:]:
        load.wait()

    def column(row):
        padded = jnp.concatenate([row, jnp.zeros((1, RPAD - RX), F32)], axis=1)
        turned = jnp.broadcast_to(padded, (BLOCK, RPAD)).T
        return turned[0:RROWS]

    for source, target in ((LP, LB), (AC, AB)):
        value = column(source[...].reshape(1, RX))
        target[:, 0:BLOCK] = value
        target[:, BLOCK:WIDE] = value

    def placed(value):
        wide = jnp.concatenate([value, jnp.zeros((SP, RPAD - RX), F32)], axis=1)
        return jnp.concatenate(
            [jnp.zeros((1, RPAD), F32), wide, jnp.zeros((CROWS - COMP, RPAD), F32)], axis=0
        )

    table = RT[...]
    first = placed(table[:, 0:RX])
    second = placed(table[:, RX : 2 * RX])
    for value, target in ((first, RA), (second, RB)):
        stacked = jnp.concatenate([value, value, value, jnp.zeros_like(value)], axis=0)
        target[...] = stacked.T[0:RROWS].astype(BF16)
    for k, value in enumerate((first, first, second, second)):
        C[:, k * RPAD : (k + 1) * RPAD] = value.astype(BF16)
    heat_row = jnp.concatenate([HT[...].reshape(1, RX), jnp.zeros((1, RPAD - RX), F32)], axis=1)
    heat_high, heat_mid, heat_low = split3(heat_row)
    row = lax.broadcasted_iota(jnp.int32, (CROWS, RPAD), 0)
    stoich = placed(PT[...])
    for at, piece in ((0, heat_high), (COMP, heat_mid), (COMP + 1, heat_low)):
        stoich = jnp.where(row == at, piece.astype(F32), stoich)
    PP[:, 0:RPAD] = stoich.astype(BF16)
    PP[:, RPAD : 2 * RPAD] = stoich.astype(BF16)
    Z[...] = jnp.zeros_like(Z)
    A[...] = jnp.zeros_like(A)

    before = jnp.zeros((8, BLOCK), jnp.int32)
    slot_plane = jnp.zeros((8, BLOCK), jnp.int32)
    slot_tile = jnp.zeros((8, BLOCK), jnp.int32) - 1
    slot_count = jnp.zeros((8, BLOCK), jnp.int32)
    burning = FL[...]
    counts = SB[...]
    for t in range(8):
        for x in range(8):
            lit = jnp.broadcast_to(burning[x : x + 1, t : t + 1], (8, BLOCK))
            steps = jnp.broadcast_to(counts[x : x + 1, t : t + 1], (8, BLOCK))
            match = (lit == 1) & (before == sub)
            slot_plane = jnp.where(match, x, slot_plane)
            slot_tile = jnp.where(match, t, slot_tile)
            slot_count = jnp.where(match, steps, slot_count)
            LV[t, x : x + 1, :] = lit[0:1]
            RK[t, x : x + 1, :] = jnp.minimum(before, SLOTS - 1)[0:1]
            before = before + lit
    step_size = 1.0 / jnp.maximum(slot_count, 1).astype(F32)
    for v in range(SLOTS):
        CN[:, v * BLOCK : (v + 1) * BLOCK] = jnp.broadcast_to(slot_count[v : v + 1], (8, BLOCK))
        ST[:, v * BLOCK : (v + 1) * BLOCK] = jnp.broadcast_to(step_size[v : v + 1], (8, BLOCK))

    def gather(c, _):
        value = jnp.zeros((8, BLOCK), F32) + 1.0
        for t in range(8):
            tile = S[c, :, t * BLOCK : (t + 1) * BLOCK]
            value = jnp.where(slot_tile == t, jnp.take_along_axis(tile, slot_plane, axis=0), value)
        Q[c] = value
        return 0

    lax.fori_loop(0, COMP, gather, 0)
    for v in range(SLOTS):
        A[0:COMP, v * BLOCK : (v + 1) * BLOCK] = Q[:, v, :]

    component = lax.broadcasted_iota(jnp.int32, (CROWS, WIDE), 0)

    def group(g, _):
        at = pl.ds(pl.multiple_of(g * WIDE, WIDE), WIDE)

        def substep(t, _):
            amounts = A[:, at]
            inverse = 1.0 / amounts[0:1]
            speeds = jnp.exp(LB[...] - AB[...] * inverse)
            pieces = split3(amounts)
            operand = jnp.concatenate([*pieces, jnp.zeros_like(pieces[0])], axis=0)
            first_side = jnp.dot(RA[...], operand, preferred_element_type=F32)
            second_side = jnp.dot(RB[...], operand, preferred_element_type=F32)
            to_first = speeds * second_side
            to_second = speeds * first_side
            progress = to_second * second_side
            for k, value in enumerate((to_first, to_second, progress)):
                high, low = split2(value)
                Z[2 * k * RPAD : 2 * k * RPAD + RROWS, :] = high
                Z[(2 * k + 1) * RPAD : (2 * k + 1) * RPAD + RROWS, :] = low
            consumed = jnp.dot(C[...], Z[0 : 4 * RPAD, :], preferred_element_type=F32)
            produced = jnp.dot(PP[...], Z[4 * RPAD : 6 * RPAD, :], preferred_element_type=F32)
            warmed = produced[0:1] + produced[COMP : COMP + 1] + produced[COMP + 1 : COMP + 2]
            produced = jnp.where(component == 0, warmed, produced)
            step = ST[0:1, at]
            updated = (amounts + step * produced) / (1.0 + step * consumed)
            active = (t < CN[0:1, at]) & (component < COMP)
            A[:, at] = jnp.where(active, updated, amounts)
            return 0

        lax.fori_loop(0, MAXSUB, substep, 0)
        return 0

    lax.fori_loop(0, SLOTS * BLOCK // WIDE, group, 0)
    for v in range(SLOTS):
        Q[:, v, :] = A[0:COMP, v * BLOCK : (v + 1) * BLOCK]

    zpos = lane % NZ

    def along_z(tile, offset):
        if offset > 0:
            return jnp.where(
                zpos < NZ - offset, pltpu.roll(tile, BLOCK - offset, 1), pltpu.roll(tile, NZ - offset, 1)
            )
        reach = -offset
        return jnp.where(zpos >= reach, pltpu.roll(tile, reach, 1), pltpu.roll(tile, BLOCK + reach - NZ, 1))

    def inner(c, _):
        weight = DF[0, c]
        done = Q[c]
        tiles = [S[c, :, t * BLOCK : (t + 1) * BLOCK] for t in range(8)]
        plus = [pltpu.roll(x, BLOCK - NZ, 1) for x in tiles]
        minus = [pltpu.roll(x, NZ, 1) for x in tiles]
        half = [pltpu.roll(x, 2 * NZ, 1) for x in tiles]
        zero = jnp.zeros((8, BLOCK), F32)
        for t, x in enumerate(tiles):
            before_y = minus[t - 1] if t > 0 else zero
            after_y = plus[t + 1] if t < 7 else zero
            before_y2 = half[t - 1] if t > 0 else zero
            after_y2 = half[t + 1] if t < 7 else zero
            near = jnp.where(lane >= NZ, minus[t], before_y) + jnp.where(lane < BLOCK - NZ, plus[t], after_y)
            far = jnp.where(lane >= 2 * NZ, half[t], before_y2) + jnp.where(lane < 2 * NZ, half[t], after_y2)
            near = near + (along_z(x, 1) + along_z(x, -1))
            far = far + (along_z(x, 2) + along_z(x, -2))
            near = near + (
                jnp.where(sub >= 1, pltpu.roll(x, 1, 0), 0.0) + jnp.where(sub < 7, pltpu.roll(x, 7, 0), 0.0)
            )
            far = far + (
                jnp.where(sub >= 2, pltpu.roll(x, 2, 0), 0.0) + jnp.where(sub < 6, pltpu.roll(x, 6, 0), 0.0)
            )
            reacted = jnp.where(LV[t] == 1, jnp.take_along_axis(done, RK[t], axis=0), x)
            out[c, :, t * BLOCK : (t + 1) * BLOCK] = reacted + weight * (
                near_weight * near - far_weight * far - centre_weight * x
            )
        return 0

    lax.fori_loop(0, COMP, inner, 0)

    for copy in y_copies:
        copy.wait_recv()

    def edges(c, _):
        low, high = YR[0, c], YR[1, c]
        for comp, lo, hi in (
            (c, low, pltpu.roll(high, 64, 1)),
            (c + HALF, pltpu.roll(low, 64, 1), high),
        ):
            weight = DF[0, comp]
            near = jnp.where(lane < NZ, pltpu.roll(lo, BLOCK - NZ, 1), 0.0)
            far = jnp.where(lane < 2 * NZ, lo, 0.0)
            out[comp, :, 0:128] += weight * (near_weight * near - far_weight * far)
            near = jnp.where(lane >= BLOCK - NZ, pltpu.roll(hi, NZ, 1), 0.0)
            far = jnp.where(lane >= 2 * NZ, hi, 0.0)
            out[comp, :, 896:1024] += weight * (near_weight * near - far_weight * far)
        return 0

    lax.fori_loop(0, HALF, edges, 0)

    sub_row = lax.broadcasted_iota(jnp.int32, (8, 1024), 0)

    def outer(c, _):
        weight = DF[0, c]
        x = H[c]
        near = jnp.where(
            sub_row == 0, pltpu.roll(x, 1, 0), jnp.where(sub_row == 7, pltpu.roll(x, 7, 0), 0.0)
        )
        far = jnp.where(
            sub_row < 2, pltpu.roll(x, 2, 0), jnp.where(sub_row >= 6, pltpu.roll(x, 6, 0), 0.0)
        )
        out[c] += weight * (near_weight * near - far_weight * far)
        return 0

    for (c0, cn), pair in zip(CHUNKS, x_copies):
        for copy in pair:
            copy.wait_recv()
        lax.fori_loop(c0, c0 + cn, outer, 0)

    for pair in x_copies:
        for copy in pair:
            copy.wait_send()
    for copy in y_copies:
        copy.wait_send()


def per_device(
    state, diffusivity, log_prefactor, activation, heat, reactants, products, substeps, flame
):
    n, m = lax.axis_size("gx"), lax.axis_size("gy")
    anywhere = pl.BlockSpec(memory_space=pl.ANY)
    vmem, smem, dma = pltpu.VMEM, pltpu.SMEM, pltpu.SemaphoreType.DMA
    cells = state.shape[2]
    return pl.pallas_call(
        functools.partial(kernel, n, m),
        out_shape=pltpu.VMEM(state.shape, F32),
        in_specs=[anywhere] * 9,
        out_specs=pl.BlockSpec(memory_space=pltpu.VMEM),
        scratch_shapes=[
            vmem((COMP, 8, cells), F32),
            vmem((COMP, 8, cells), F32),
            vmem((2, HALF, 8, BLOCK), F32),
            vmem((2, HALF, 8, BLOCK), F32),
            smem((1, COMP), F32),
            vmem((RX,), F32),
            vmem((RX,), F32),
            vmem((RX,), F32),
            vmem((SP, 2 * RX), F32),
            vmem((SP, RX), F32),
            vmem((8, 8), jnp.int32),
            vmem((8, 8), jnp.int32),
            vmem((RROWS, WIDE), F32),
            vmem((RROWS, WIDE), F32),
            vmem((RROWS, 4 * CROWS), BF16),
            vmem((RROWS, 4 * CROWS), BF16),
            vmem((CROWS, 4 * RPAD), BF16),
            vmem((CROWS, 2 * RPAD), BF16),
            vmem((CROWS, SLOTS * BLOCK), F32),
            vmem((COMP, SLOTS, BLOCK), F32),
            vmem((8, SLOTS * BLOCK), jnp.int32),
            vmem((8, SLOTS * BLOCK), F32),
            vmem((6 * RPAD, WIDE), BF16),
            vmem((8, 8, BLOCK), jnp.int32),
            vmem((8, 8, BLOCK), jnp.int32),
            dma((2, len(CHUNKS))), dma((2, len(CHUNKS))), dma((2,)), dma((2,)), dma((9,)),
        ],
        compiler_params=pltpu.CompilerParams(
            collective_id=0, has_side_effects=True, vmem_limit_bytes=VMEM_LIMIT
        ),
    )(
        state, diffusivity.reshape(1, -1), log_prefactor, activation,
        heat, reactants.T, products, substeps, flame,
    )


VMEM_LIMIT = 60 << 20


def solution(mesh):
    in_specs = (P(None, "gx", "gy"), P(), P(), P(), P(), P(), P(), P("gx", "gy"), P("gx", "gy"))
    return jax.shard_map(
        per_device, mesh=mesh, in_specs=in_specs, out_specs=P(None, "gx", "gy"), check_vma=False
    )
```

time: 108 us -> 67.2 us (0.62)
  the two profiles are of different devices: /device:TPU:67 before, /device:TPU:1 now
where the time goes in v1:
time: 67.2 us; the launch traced here: 67 us
  Pallas kernels  65.8 us (98%)
  local copies, waits for them, and re-layouts  1.21 us (2%)
    pallas_call x1, Pallas kernels, per_device(): pl.pallas_call(functools.partial(kernel, n, m), out_shape=pltpu.VMEM(stat...  65.8 us

profile of v1, /device:TPU:1, one launch (start us, length us, event | category | flops | bytes accessed | tf_op | source)
XLA Modules:
  0.0 67.0 jit_solution(5200543158313745757)
XLA Ops:
  0.0 65.8 %shard_map.91 = f32[54,8,1024]{2,1,0:T(8,128)S(1)} custom-call(f32[54,8,1024]{2,1,0:T(8,128)} %state.1, f32[1,54]{1,0:T(1,128)} %bitcast.3, f32[325]{0:T(512)} %log_prefactor.1, f32[325]{0:T(512)} %activation.1, f32[325]{0:T(512)} %heat.1, f32[53,650]{1,0:T(8,128)} %bitcast.2, f32[53,325]{1,0:T(8,128)} %products.1, s32[8,8]{1,0:T(8,128)} %substeps.1, ...), custom_call_target="tpu_custom_call" | custom-call | tf_op jit(solution)/shard_map/pallas_call | solution.py:324
  65.8 1.2 %copy.11 = f32[54,8,1024]{2,1,0:T(8,128)} copy(f32[54,8,1024]{2,1,0:T(8,128)S(1)} %shard_map.91) | data formatting | bytes 3538944

commit v2 on v1

--- a/solution.py
+++ b/solution.py
@@ -42,6 +42,15 @@
     return high, middle, (rest - middle.astype(F32)).astype(BF16)
 
 
+def looped(first, count, body, together):
+    def step(i, _):
+        for k in range(together):
+            body(first + i * together + k, 0)
+        return 0
+
+    lax.fori_loop(0, count // together, step, 0)
+
+
 def kernel(
     n, m,
     state, diffusivity, log_prefactor, activation, heat, reactants_t, products, substeps, flame,
@@ -55,8 +64,22 @@
     up, down = lax.rem(gy + 1, m), lax.rem(gy + m - 1, m)
 
     barrier = pltpu.get_barrier_semaphore()
-    for device in ((right, gy), (left, gy), (gx, up), (gx, down)):
+    part = lax.rem(gx, 3)
+
+    def greet(device):
         pl.semaphore_signal(barrier, inc=1, device_id=device, device_id_type=MESH)
+
+    greet((gx, up))
+    greet((gx, down))
+
+    @pl.when(part == 0)
+    def _():
+        greet((right, gy))
+
+    @pl.when(part == 1)
+    def _():
+        greet((left, gy))
+
 
     loads = [
         pltpu.make_async_copy(state, S, local.at[0]),
@@ -72,7 +95,22 @@
     for load in loads:
         load.start()
 
-    pl.semaphore_wait(barrier, 4)
+    @pl.when(part == 0)
+    def _():
+        pl.semaphore_wait(barrier, 3)
+        greet((left, gy))
+
+    @pl.when(part == 1)
+    def _():
+        pl.semaphore_wait(barrier, 3)
+        greet((right, gy))
+
+    @pl.when(part == 2)
+    def _():
+        pl.semaphore_wait(barrier, 4)
+        greet((right, gy))
+        greet((left, gy))
+
     x_copies = []
     for k, (c0, cn) in enumerate(CHUNKS):
         pair = (
@@ -85,9 +123,25 @@
                 x_send.at[1, k], x_recv.at[1, k], device_id=(left, gy), device_id_type=MESH,
             ),
         )
-        for copy in pair:
-            copy.start()
         x_copies.append(pair)
+
+    place = gy // 2
+
+    @pl.when((part == 1) & (place < 3))
+    def _():
+        x_copies[0][1].start()
+        x_copies[1][1].start()
+
+    @pl.when((part == 2) & (place < 3))
+    def _():
+        x_copies[0][0].start()
+        x_copies[1][0].start()
+        x_copies[0][1].start()
+
+    @pl.when((part == 2) & (place == 3))
+    def _():
+        x_copies[0][1].start()
+
     loads[0].wait()
     lane = lax.broadcasted_iota(jnp.int32, (8, BLOCK), 1)
     sub = lax.broadcasted_iota(jnp.int32, (8, BLOCK), 0)
@@ -105,7 +159,7 @@
         )
         return 0
 
-    lax.fori_loop(0, HALF, pack, 0)
+    looped(0, HALF, pack, 3)
 
     y_copies = [
         pltpu.make_async_remote_copy(
@@ -115,8 +169,102 @@
             YS.at[1], YR.at[1], y_send.at[1], y_recv.at[1], device_id=(gx, down), device_id_type=MESH
         ),
     ]
-    for copy in y_copies:
-        copy.start()
+    @pl.when(part == 0)
+    def _():
+        y_copies[0].start()
+        y_copies[1].start()
+        x_copies[0][0].start()
+        x_copies[1][0].start()
+        x_copies[2][0].start()
+        x_copies[3][0].start()
+        x_copies[4][0].start()
+        x_copies[5][0].start()
+
+    @pl.when((part == 1) & (place < 3))
+    def _():
+        y_copies[0].start()
+        y_copies[1].start()
+        x_copies[2][1].start()
+        x_copies[3][1].start()
+        x_copies[4][1].start()
+        x_copies[5][1].start()
+
+    @pl.when((part == 1) & (place == 3))
+    def _():
+        y_copies[0].start()
+        y_copies[1].start()
+
+    @pl.when((part == 2) & (place < 3))
+    def _():
+        y_copies[0].start()
+        y_copies[1].start()
+        x_copies[2][0].start()
+        x_copies[1][1].start()
+        x_copies[3][0].start()
+        x_copies[2][1].start()
+        x_copies[4][0].start()
+        x_copies[3][1].start()
+        x_copies[5][0].start()
+        x_copies[4][1].start()
+        x_copies[5][1].start()
+
+    @pl.when((part == 2) & (place == 3))
+    def _():
+        y_copies[0].start()
+        y_copies[1].start()
+        x_copies[1][1].start()
+        x_copies[2][1].start()
+        x_copies[3][1].start()
+        x_copies[4][1].start()
+        x_copies[5][1].start()
+
+    @pl.when(part < 2)
+    def _():
+        pl.semaphore_wait(barrier, 1)
+
+    @pl.when(part == 0)
+    def _():
+        x_copies[0][1].start()
+        x_copies[1][1].start()
+        x_copies[2][1].start()
+        x_copies[3][1].start()
+        x_copies[4][1].start()
+        x_copies[5][1].start()
+
+    @pl.when((part == 1) & (place < 3))
+    def _():
+        x_copies[0][0].start()
+        x_copies[1][0].start()
+        x_copies[2][0].start()
+        x_copies[3][0].start()
+        x_copies[4][0].start()
+        x_copies[5][0].start()
+
+    def checkpoint(at):
+
+        @pl.when(((part == 2) & (place == 3)) & (at == 17))
+        def _():
+            x_copies[0][0].start()
+            x_copies[1][0].start()
+            x_copies[2][0].start()
+            x_copies[3][0].start()
+            x_copies[4][0].start()
+            x_copies[5][0].start()
+
+        @pl.when(((part == 1) & (place == 3)) & (at == 13))
+        def _():
+            x_copies[0][1].start()
+            x_copies[1][1].start()
+            x_copies[2][1].start()
+            x_copies[3][1].start()
+            x_copies[4][1].start()
+            x_copies[5][1].start()
+            x_copies[0][0].start()
+            x_copies[1][0].start()
+            x_copies[2][0].start()
+            x_copies[3][0].start()
+            x_copies[4][0].start()
+            x_copies[5][0].start()
 
     for load in loads[1:]:
         load.wait()
@@ -186,7 +334,7 @@
         Q[c] = value
         return 0
 
-    lax.fori_loop(0, COMP, gather, 0)
+    looped(0, COMP, gather, 2)
     for v in range(SLOTS):
         A[0:COMP, v * BLOCK : (v + 1) * BLOCK] = Q[:, v, :]
 
@@ -216,6 +364,7 @@
             produced = jnp.where(component == 0, warmed, produced)
             step = ST[0:1, at]
             updated = (amounts + step * produced) / (1.0 + step * consumed)
+            checkpoint(1 + MAXSUB * g + t)
             active = (t < CN[0:1, at]) & (component < COMP)
             A[:, at] = jnp.where(active, updated, amounts)
             return 0
@@ -238,6 +387,7 @@
         return jnp.where(zpos >= reach, pltpu.roll(tile, reach, 1), pltpu.roll(tile, BLOCK + reach - NZ, 1))
 
     def inner(c, _):
+        checkpoint(17 + c)
         weight = DF[0, c]
         done = Q[c]
         tiles = [S[c, :, t * BLOCK : (t + 1) * BLOCK] for t in range(8)]
@@ -266,7 +416,7 @@
             )
         return 0
 
-    lax.fori_loop(0, COMP, inner, 0)
+    looped(0, COMP, inner, 2)
 
     for copy in y_copies:
         copy.wait_recv()
@@ -286,7 +436,7 @@
             out[comp, :, 896:1024] += weight * (near_weight * near - far_weight * far)
         return 0
 
-    lax.fori_loop(0, HALF, edges, 0)
+    looped(0, HALF, edges, 3)
 
     sub_row = lax.broadcasted_iota(jnp.int32, (8, 1024), 0)
 
@@ -305,7 +455,7 @@
     for (c0, cn), pair in zip(CHUNKS, x_copies):
         for copy in pair:
             copy.wait_recv()
-        lax.fori_loop(c0, c0 + cn, outer, 0)
+        looped(c0, cn, outer, 3)
 
     for pair in x_copies:
         for copy in pair:

time: 67.2 us -> 59.6 us (0.89)
  the two profiles are of different devices: /device:TPU:1 before, /device:TPU:193 now
where the time goes in v2:
time: 59.6 us; the launch traced here: 59.5 us
  Pallas kernels  58.2 us (98%)
  local copies, waits for them, and re-layouts  1.21 us (2%)
    pallas_call x1, Pallas kernels, per_device(): pl.pallas_call(functools.partial(kernel, n, m), out_shape=pltpu.VMEM(stat...  58.2 us
    unnamed x1, local copies, waits for them, and re-layouts  1.21 us

profile of v2, /device:TPU:193, one launch (start us, length us, event | category | flops | bytes accessed | tf_op | source)
XLA Modules:
  0.0 59.5 jit_solution(3139680249929309835)
XLA Ops:
  0.0 58.2 %shard_map.91 = f32[54,8,1024]{2,1,0:T(8,128)S(1)} custom-call(f32[54,8,1024]{2,1,0:T(8,128)} %state.1, f32[1,54]{1,0:T(1,128)} %bitcast.3, f32[325]{0:T(512)} %log_prefactor.1, f32[325]{0:T(512)} %activation.1, f32[325]{0:T(512)} %heat.1, f32[53,650]{1,0:T(8,128)} %bitcast.2, f32[53,325]{1,0:T(8,128)} %products.1, s32[8,8]{1,0:T(8,128)} %substeps.1, ...), custom_call_target="tpu_custom_call" | custom-call | tf_op jit(solution)/shard_map/pallas_call | solution.py:474
  58.2 1.2 %copy.11 = f32[54,8,1024]{2,1,0:T(8,128)} copy(f32[54,8,1024]{2,1,0:T(8,128)S(1)} %shard_map.91) | data formatting | bytes 3538944

commit v3 on v1

--- a/solution.py
+++ b/solution.py
@@ -42,21 +42,51 @@
     return high, middle, (rest - middle.astype(F32)).astype(BF16)
 
 
+def looped(first, count, body, together):
+    def step(i, _):
+        for k in range(together):
+            body(first + i * together + k, 0)
+        return 0
+
+    lax.fori_loop(0, count // together, step, 0)
+
+
 def kernel(
     n, m,
     state, diffusivity, log_prefactor, activation, heat, reactants_t, products, substeps, flame,
     out,
     S, H, YS, YR, DF, LP, AC, HT, RT, PT, SB, FL,
     LB, AB, RA, RB, C, PP, A, Q, CN, ST, Z, LV, RK,
-    x_send, x_recv, y_send, y_recv, local,
+    x_send, x_recv, y_send, y_recv, local, from_right, from_left, from_up, from_down,
 ):
     gx, gy = lax.axis_index("gx"), lax.axis_index("gy")
     right, left = lax.rem(gx + 1, n), lax.rem(gx + n - 1, n)
     up, down = lax.rem(gy + 1, m), lax.rem(gy + m - 1, m)
 
     barrier = pltpu.get_barrier_semaphore()
-    for device in ((right, gy), (left, gy), (gx, up), (gx, down)):
-        pl.semaphore_signal(barrier, inc=1, device_id=device, device_id_type=MESH)
+    part = lax.rem(gx, 3)
+    place = gy // 2
+
+    def tell(semaphore, device):
+        pl.semaphore_signal(semaphore, inc=1, device_id=device, device_id_type=MESH)
+
+    @pl.when(part == 0)
+    def _():
+        tell(barrier, (right, gy))
+        tell(barrier, (left, gy))
+
+    @pl.when(part == 1)
+    def _():
+        tell(barrier, (right, gy))
+
+    @pl.when(gy < m - 1)
+    def _():
+        tell(barrier, (gx, up))
+
+    @pl.when(gy == 0)
+    def _():
+        tell(barrier, (gx, down))
+
 
     loads = [
         pltpu.make_async_copy(state, S, local.at[0]),
@@ -72,7 +102,26 @@
     for load in loads:
         load.start()
 
-    pl.semaphore_wait(barrier, 4)
+    @pl.when(part + gy > 0)
+    def _():
+        pl.semaphore_wait(barrier, part + (gy + m - 2) // (m - 1) + gy // (m - 1))
+
+    @pl.when(part >= 1)
+    def _():
+        tell(from_right, (left, gy))
+
+    @pl.when(part == 2)
+    def _():
+        tell(from_left, (right, gy))
+
+    @pl.when(gy >= 1)
+    def _():
+        tell(from_up, (gx, down))
+
+    @pl.when(gy == m - 1)
+    def _():
+        tell(from_down, (gx, up))
+
     x_copies = []
     for k, (c0, cn) in enumerate(CHUNKS):
         pair = (
@@ -85,9 +134,19 @@
                 x_send.at[1, k], x_recv.at[1, k], device_id=(left, gy), device_id_type=MESH,
             ),
         )
-        for copy in pair:
-            copy.start()
         x_copies.append(pair)
+
+    @pl.when(part == 2)
+    def _():
+        x_copies[0][0].start()
+        x_copies[1][0].start()
+        x_copies[0][1].start()
+
+    @pl.when(part == 1)
+    def _():
+        x_copies[0][1].start()
+        x_copies[1][1].start()
+
     loads[0].wait()
     lane = lax.broadcasted_iota(jnp.int32, (8, BLOCK), 1)
     sub = lax.broadcasted_iota(jnp.int32, (8, BLOCK), 0)
@@ -105,7 +164,7 @@
         )
         return 0
 
-    lax.fori_loop(0, HALF, pack, 0)
+    looped(0, HALF, pack, 3)
 
     y_copies = [
         pltpu.make_async_remote_copy(
@@ -115,8 +174,77 @@
             YS.at[1], YR.at[1], y_send.at[1], y_recv.at[1], device_id=(gx, down), device_id_type=MESH
         ),
     ]
-    for copy in y_copies:
-        copy.start()
+    @pl.when(gy >= 1)
+    def _():
+        y_copies[1].start()
+
+    @pl.when(gy == m - 1)
+    def _():
+        y_copies[0].start()
+
+    @pl.when(part == 2)
+    def _():
+        x_copies[2][0].start()
+        x_copies[1][1].start()
+        x_copies[3][0].start()
+        x_copies[2][1].start()
+        x_copies[4][0].start()
+        x_copies[3][1].start()
+        x_copies[5][0].start()
+        x_copies[4][1].start()
+        x_copies[5][1].start()
+
+    @pl.when(part == 1)
+    def _():
+        x_copies[2][1].start()
+        x_copies[3][1].start()
+        x_copies[4][1].start()
+        x_copies[5][1].start()
+
+    @pl.when(gy < m - 1)
+    def _():
+        pl.semaphore_wait(from_up, 1)
+        y_copies[0].start()
+
+    @pl.when(gy == 0)
+    def _():
+        pl.semaphore_wait(from_down, 1)
+        y_copies[1].start()
+
+    @pl.when(part <= 1)
+    def _():
+        pl.semaphore_wait(from_right, 1)
+
+    @pl.when(part == 0)
+    def _():
+        x_copies[0][0].start()
+        x_copies[1][0].start()
+        x_copies[2][0].start()
+        x_copies[3][0].start()
+        x_copies[4][0].start()
+        x_copies[5][0].start()
+
+    @pl.when(part == 1)
+    def _():
+        x_copies[0][0].start()
+        x_copies[1][0].start()
+        x_copies[2][0].start()
+        x_copies[3][0].start()
+        x_copies[4][0].start()
+        x_copies[5][0].start()
+
+    @pl.when(part == 0)
+    def _():
+        pl.semaphore_wait(from_left, 1)
+
+    @pl.when(part == 0)
+    def _():
+        x_copies[0][1].start()
+        x_copies[1][1].start()
+        x_copies[2][1].start()
+        x_copies[3][1].start()
+        x_copies[4][1].start()
+        x_copies[5][1].start()
 
     for load in loads[1:]:
         load.wait()
@@ -186,7 +314,7 @@
         Q[c] = value
         return 0
 
-    lax.fori_loop(0, COMP, gather, 0)
+    looped(0, COMP, gather, 2)
     for v in range(SLOTS):
         A[0:COMP, v * BLOCK : (v + 1) * BLOCK] = Q[:, v, :]
 
@@ -266,7 +394,7 @@
             )
         return 0
 
-    lax.fori_loop(0, COMP, inner, 0)
+    looped(0, COMP, inner, 2)
 
     for copy in y_copies:
         copy.wait_recv()
@@ -286,7 +414,7 @@
             out[comp, :, 896:1024] += weight * (near_weight * near - far_weight * far)
         return 0
 
-    lax.fori_loop(0, HALF, edges, 0)
+    looped(0, HALF, edges, 3)
 
     sub_row = lax.broadcasted_iota(jnp.int32, (8, 1024), 0)
 
@@ -305,7 +433,7 @@
     for (c0, cn), pair in zip(CHUNKS, x_copies):
         for copy in pair:
             copy.wait_recv()
-        lax.fori_loop(c0, c0 + cn, outer, 0)
+        looped(c0, cn, outer, 3)
 
     for pair in x_copies:
         for copy in pair:
@@ -353,6 +481,7 @@
             vmem((8, 8, BLOCK), jnp.int32),
             vmem((8, 8, BLOCK), jnp.int32),
             dma((2, len(CHUNKS))), dma((2, len(CHUNKS))), dma((2,)), dma((2,)), dma((9,)),
+            *[pltpu.SemaphoreType.REGULAR] * 4,
         ],
         compiler_params=pltpu.CompilerParams(
             collective_id=0, has_side_effects=True, vmem_limit_bytes=VMEM_LIMIT

time: 67.2 us -> 57.3 us (0.85)
  the two profiles are of different devices: /device:TPU:1 before, /device:TPU:193 now
where the time goes in v3:
time: 57.3 us; the launch traced here: 57.2 us
  Pallas kernels  56 us (98%)
  local copies, waits for them, and re-layouts  1.21 us (2%)
    pallas_call x1, Pallas kernels, per_device(): pl.pallas_call(functools.partial(kernel, n, m), out_shape=pltpu.VMEM(stat...  56 us
    unnamed x1, local copies, waits for them, and re-layouts  1.21 us

profile of v3, /device:TPU:193, one launch (start us, length us, event | category | flops | bytes accessed | tf_op | source)
XLA Modules:
  0.0 57.2 jit_solution(8482044602495673187)
XLA Ops:
  0.0 56.0 %shard_map.91 = f32[54,8,1024]{2,1,0:T(8,128)S(1)} custom-call(f32[54,8,1024]{2,1,0:T(8,128)} %state.1, f32[1,54]{1,0:T(1,128)} %bitcast.3, f32[325]{0:T(512)} %log_prefactor.1, f32[325]{0:T(512)} %activation.1, f32[325]{0:T(512)} %heat.1, f32[53,650]{1,0:T(8,128)} %bitcast.2, f32[53,325]{1,0:T(8,128)} %products.1, s32[8,8]{1,0:T(8,128)} %substeps.1, ...), custom_call_target="tpu_custom_call" | custom-call | tf_op jit(solution)/shard_map/pallas_call | solution.py:452
  56.0 1.2 %copy.11 = f32[54,8,1024]{2,1,0:T(8,128)} copy(f32[54,8,1024]{2,1,0:T(8,128)S(1)} %shard_map.91) | data formatting | bytes 3538944

commit v4 on v3

--- a/solution.py
+++ b/solution.py
@@ -19,7 +19,7 @@
 RPAD = 384
 WIDE = 256
 HALF = COMP // 2
-CHUNKS = ((0, 9), (9, 9), (18, 9), (27, 9), (36, 9), (45, 9))
+CHUNKS = ((0, 12), (12, 12), (24, 12), (36, 9), (45, 6), (51, 3))
 
 near_weight = 4.0 / 3.0
 far_weight = 1.0 / 12.0
@@ -87,6 +87,59 @@
     def _():
         tell(barrier, (gx, down))
 
+
+    @pl.when(part + gy > 0)
+    def _():
+        pl.semaphore_wait(barrier, part + (gy + m - 2) // (m - 1) + gy // (m - 1))
+
+    @pl.when(part >= 1)
+    def _():
+        tell(from_right, (left, gy))
+
+    @pl.when(part == 2)
+    def _():
+        tell(from_left, (right, gy))
+
+    @pl.when(gy >= 1)
+    def _():
+        tell(from_up, (gx, down))
+
+    @pl.when(gy == m - 1)
+    def _():
+        tell(from_down, (gx, up))
+
+    x_copies = []
+    for k, (c0, cn) in enumerate(CHUNKS):
+        pair = (
+            pltpu.make_async_remote_copy(
+                state.at[c0 : c0 + cn, 6:8, :], H.at[c0 : c0 + cn, 6:8, :],
+                x_send.at[0, k], x_recv.at[0, k], device_id=(right, gy), device_id_type=MESH,
+            ),
+            pltpu.make_async_remote_copy(
+                state.at[c0 : c0 + cn, 0:2, :], H.at[c0 : c0 + cn, 0:2, :],
+                x_send.at[1, k], x_recv.at[1, k], device_id=(left, gy), device_id_type=MESH,
+            ),
+        )
+        x_copies.append(pair)
+
+    @pl.when(part == 2)
+    def _():
+        x_copies[0][0].start()
+        x_copies[1][0].start()
+        x_copies[2][0].start()
+        x_copies[3][0].start()
+        x_copies[4][0].start()
+        x_copies[5][0].start()
+        x_copies[0][1].start()
+
+    @pl.when(part == 1)
+    def _():
+        x_copies[0][1].start()
+        x_copies[1][1].start()
+        x_copies[2][1].start()
+        x_copies[3][1].start()
+        x_copies[4][1].start()
+        x_copies[5][1].start()
 
     loads = [
         pltpu.make_async_copy(state, S, local.at[0]),
@@ -102,51 +155,6 @@
     for load in loads:
         load.start()
 
-    @pl.when(part + gy > 0)
-    def _():
-        pl.semaphore_wait(barrier, part + (gy + m - 2) // (m - 1) + gy // (m - 1))
-
-    @pl.when(part >= 1)
-    def _():
-        tell(from_right, (left, gy))
-
-    @pl.when(part == 2)
-    def _():
-        tell(from_left, (right, gy))
-
-    @pl.when(gy >= 1)
-    def _():
-        tell(from_up, (gx, down))
-
-    @pl.when(gy == m - 1)
-    def _():
-        tell(from_down, (gx, up))
-
-    x_copies = []
-    for k, (c0, cn) in enumerate(CHUNKS):
-        pair = (
-            pltpu.make_async_remote_copy(
-                state.at[c0 : c0 + cn, 6:8, :], H.at[c0 : c0 + cn, 6:8, :],
-                x_send.at[0, k], x_recv.at[0, k], device_id=(right, gy), device_id_type=MESH,
-            ),
-            pltpu.make_async_remote_copy(
-                state.at[c0 : c0 + cn, 0:2, :], H.at[c0 : c0 + cn, 0:2, :],
-                x_send.at[1, k], x_recv.at[1, k], device_id=(left, gy), device_id_type=MESH,
-            ),
-        )
-        x_copies.append(pair)
-
-    @pl.when(part == 2)
-    def _():
-        x_copies[0][0].start()
-        x_copies[1][0].start()
-        x_copies[0][1].start()
-
-    @pl.when(part == 1)
-    def _():
-        x_copies[0][1].start()
-        x_copies[1][1].start()
-
     loads[0].wait()
     lane = lax.broadcasted_iota(jnp.int32, (8, BLOCK), 1)
     sub = lax.broadcasted_iota(jnp.int32, (8, BLOCK), 0)
@@ -184,18 +192,7 @@
 
     @pl.when(part == 2)
     def _():
-        x_copies[2][0].start()
         x_copies[1][1].start()
-        x_copies[3][0].start()
-        x_copies[2][1].start()
-        x_copies[4][0].start()
-        x_copies[3][1].start()
-        x_copies[5][0].start()
-        x_copies[4][1].start()
-        x_copies[5][1].start()
-
-    @pl.when(part == 1)
-    def _():
         x_copies[2][1].start()
         x_copies[3][1].start()
         x_copies[4][1].start()

time: 57.3 us -> 57.2 us (level)
  no operation moved by 1% of the time
where the time goes in v4:
time: 57.2 us; the launch traced here: 57.1 us
  Pallas kernels  55.9 us (98%)
  local copies, waits for them, and re-layouts  1.21 us (2%)
    pallas_call x1, Pallas kernels, per_device(): pl.pallas_call(functools.partial(kernel, n, m), out_shape=pltpu.VMEM(stat...  55.9 us
    unnamed x1, local copies, waits for them, and re-layouts  1.21 us

profile of v4, /device:TPU:193, one launch (start us, length us, event | category | flops | bytes accessed | tf_op | source)
XLA Modules:
  0.0 57.1 jit_solution(6327487058903729933)
XLA Ops:
  0.0 55.9 %shard_map.91 = f32[54,8,1024]{2,1,0:T(8,128)S(1)} custom-call(f32[54,8,1024]{2,1,0:T(8,128)} %state.1, f32[1,54]{1,0:T(1,128)} %bitcast.3, f32[325]{0:T(512)} %log_prefactor.1, f32[325]{0:T(512)} %activation.1, f32[325]{0:T(512)} %heat.1, f32[53,650]{1,0:T(8,128)} %bitcast.2, f32[53,325]{1,0:T(8,128)} %products.1, s32[8,8]{1,0:T(8,128)} %substeps.1, ...), custom_call_target="tpu_custom_call" | custom-call | tf_op jit(solution)/shard_map/pallas_call | solution.py:449
  55.9 1.2 %copy.11 = f32[54,8,1024]{2,1,0:T(8,128)} copy(f32[54,8,1024]{2,1,0:T(8,128)S(1)} %shard_map.91) | data formatting | bytes 3538944
